TPU v7x, 32 devices: a whole 2x2x4 slice. The times are simulated.
32 devices in a mesh: slab: 8 (over z, x), freq: 4 (over y, core).
Axes of the slice: x: 2, y: 2, z: 4, core: 2. Of those that a mesh axis runs over, the one named last changes fastest.
Arguments:
- source: bfloat16 [4, 2, 3, 64, 64, 128], P('freq', None, None, 'slab'), may hold values from -6 to 6
- omega: float32 [4], P('freq'), may hold values from 0.2 to 5
- sigma_blocks: float32 [256], replicated, may hold values from 0.25 to 4
- block_ids: int32 [64, 64, 128], P('slab'), may hold values from 0 to 255
- rec_owner: int32 [1024, 1], P('slab'), may hold values from 0 to 7; in each aligned block of 128 rows (0 to 127, 128 to 255, ...) at most 32 rows name the same one
- rec_edge: int32 [1024], P('slab'), may hold values from 0 to 196607
- observed: float32 [4, 2, 1024], P('freq', None, 'slab'), may hold values from -4 to 4
Outputs:
- forward_field: float32 [4, 2, 3, 64, 64, 128], P('freq', None, None, 'slab')
- adjoint_field: float32 [4, 2, 3, 64, 64, 128], P('freq', None, None, 'slab')
- gradient: float32 [256], replicated
Inputs may be any that keep to these rules, and one draw needn't show every extreme that they name: `rec_owner`: among the receiver rows of one slab device no slab is named more than 32 times; in some device's rows one slab is named exactly 32 times.
All inputs are finite; a program needn't handle non-finite values.
Results may differ from a plain program's by a relative error of at most 0.0003.
Values sent between devices are 32-bit elements; how exact they have to be, the bound alone decides.
A program may use at most 256 MiB of HBM per device.

v0:
```python
import jax
import jax.numpy as jnp
from jax import lax
from jax.sharding import PartitionSpec as P

SWEEPS = 4
epsilon = 1e-06


def extended(cells, sides, width):
    for axis, dim in sides:
        count = lax.axis_size(axis)
        ends = count - 1
        head = lax.slice_in_dim(cells, 0, width, axis=dim)
        tail = lax.slice_in_dim(cells, cells.shape[dim] - width, cells.shape[dim], axis=dim)
        cells = jnp.concatenate(
            [
                lax.ppermute(tail, axis, [(i, (i + 1) % count) for i in range(ends)]),
                cells,
                lax.ppermute(head, axis, [((i + 1) % count, i) for i in range(ends)]),
            ],
            axis=dim,
        )
    return cells


def forward_diff(values, along):
    along = along % values.ndim
    count = values.shape[along]
    ahead_values = jnp.concatenate(
        [
            lax.slice_in_dim(values, 1, count, axis=along),
            jnp.zeros_like(lax.slice_in_dim(values, 0, 1, axis=along)),
        ],
        axis=along,
    )
    return ahead_values - values


def adjoint_diff(values, along):
    along = along % values.ndim
    count = values.shape[along]
    behind = jnp.concatenate(
        [
            jnp.zeros_like(lax.slice_in_dim(values, 0, 1, axis=along)),
            lax.slice_in_dim(values, 0, count - 1, axis=along),
        ],
        axis=along,
    )
    return behind - values


def stiffness_of(field):
    padded = extended(field, (("slab", 3),), 1)
    edge_first = padded[:, :, 0]
    edge_second = padded[:, :, 1]
    edge_third = padded[:, :, 2]
    curl_first = forward_diff(edge_third[:, :, 1:-1], -2) - forward_diff(
        edge_second[:, :, 1:-1], -1
    )
    full_second = forward_diff(edge_first[:, :, :-1], -1) - (
        edge_third[:, :, 1:] - edge_third[:, :, :-1]
    )
    full_third = (
        edge_second[:, :, 1:] - edge_second[:, :, :-1] - forward_diff(edge_first[:, :, :-1], -2)
    )
    lower_valid = (lax.axis_index("slab") > 0).astype(jnp.float32)
    curl_second = jnp.concatenate(
        [full_second[:, :, :1] * lower_valid, full_second[:, :, 1:]], axis=2
    )
    curl_third = jnp.concatenate([full_third[:, :, :1] * lower_valid, full_third[:, :, 1:]], axis=2)
    back_first = adjoint_diff(curl_second[:, :, 1:], -1) - adjoint_diff(curl_third[:, :, 1:], -2)
    back_second = curl_third[:, :, :-1] - curl_third[:, :, 1:] - adjoint_diff(curl_first, -1)
    back_third = adjoint_diff(curl_first, -2) - (curl_second[:, :, :-1] - curl_second[:, :, 1:])
    return jnp.stack([back_first, back_second, back_third], axis=2)


def residual_sweeps(right_side, damping):
    denominator = 16.0 + damping * damping
    residual = right_side
    solution = jnp.zeros_like(right_side)
    for iteration in range(SWEEPS):
        residual_real = residual[:, 0]
        residual_imag = residual[:, 1]
        precond_real = (4.0 * residual_real + damping * residual_imag) / denominator
        precond_imag = (4.0 * residual_imag - damping * residual_real) / denominator
        stiffness = stiffness_of(jnp.stack([precond_real, precond_imag], axis=1))
        image_real = stiffness[:, 0] - damping * precond_imag
        image_imag = stiffness[:, 1] + damping * precond_real
        totals = lax.psum(
            (
                jnp.sum(image_real * residual_real + image_imag * residual_imag, axis=(1, 2, 3, 4)),
                jnp.sum(image_real * residual_imag - image_imag * residual_real, axis=(1, 2, 3, 4)),
                jnp.sum(image_real * image_real + image_imag * image_imag, axis=(1, 2, 3, 4)),
            ),
            "slab",
        )
        lower_sum = totals[2] + epsilon
        step_real = (totals[0] / lower_sum)[:, None, None, None, None]
        step_imag = (totals[1] / lower_sum)[:, None, None, None, None]
        solution = solution + jnp.stack(
            [
                step_real * precond_real - step_imag * precond_imag,
                step_real * precond_imag + step_imag * precond_real,
            ],
            axis=1,
        )
        residual = residual - jnp.stack(
            [
                step_real * image_real - step_imag * image_imag,
                step_real * image_imag + step_imag * image_real,
            ],
            axis=1,
        )
    return solution


def body(source, omega, sigma_blocks, block_ids, rec_owner, rec_edge, observed):
    conductivity = jnp.take(sigma_blocks, block_ids, axis=0)
    damping = omega[:, None, None, None, None] * conductivity[None, None]
    forward_field = residual_sweeps(source.astype(jnp.float32), damping)
    pair_count = forward_field.shape[0]
    flat_field = forward_field.reshape(pair_count, 2, -1)
    slab_count = lax.axis_size("slab")
    owner_slab = rec_owner[:, 0]
    local_count = rec_edge.shape[0]
    owner_hits = (owner_slab[:, None] == jnp.arange(slab_count, dtype=jnp.int32)[None, :]).astype(
        jnp.int32
    )
    earlier = jnp.cumsum(owner_hits, axis=0) - owner_hits
    slot_index = jnp.sum(earlier * owner_hits, axis=1)
    capacity = local_count // 4
    target = owner_slab * capacity + slot_index
    request = (
        jnp.full((slab_count * capacity,), -1, jnp.int32)
        .at[target]
        .set(rec_edge)
        .reshape(slab_count, capacity)
    )
    arrived = lax.all_to_all(request, "slab", split_axis=0, concat_axis=0, tiled=True)
    wanted = arrived.reshape(-1)
    present = (wanted >= 0).astype(jnp.float32)
    safe_edge = jnp.maximum(wanted, 0)
    picked = (jnp.take(flat_field, safe_edge, axis=2) * present).reshape(
        pair_count, 2, slab_count, capacity
    )
    returned = lax.all_to_all(picked, "slab", split_axis=2, concat_axis=2, tiled=True)
    predicted = jnp.take(returned.reshape(pair_count, 2, -1), target, axis=2)
    misfit = predicted - observed
    adjoint_data = jnp.stack([misfit[:, 0], -misfit[:, 1]], axis=1)
    outgoing = (
        jnp.zeros((pair_count, 2, slab_count * capacity), jnp.float32)
        .at[:, :, target]
        .set(adjoint_data)
        .reshape(pair_count, 2, slab_count, capacity)
    )
    incoming = lax.all_to_all(outgoing, "slab", split_axis=2, concat_axis=2, tiled=True)
    adjoint_flat = (
        jnp.zeros_like(flat_field)
        .at[:, :, safe_edge]
        .add(incoming.reshape(pair_count, 2, -1) * present)
    )
    adjoint_field = residual_sweeps(adjoint_flat.reshape(forward_field.shape), damping)
    cell_term = jnp.sum(
        omega[:, None, None, None]
        * jnp.sum(
            adjoint_field[:, 0] * forward_field[:, 1] + adjoint_field[:, 1] * forward_field[:, 0],
            axis=1,
        ),
        axis=0,
    )
    local_terms = jax.ops.segment_sum(
        cell_term.reshape(-1), block_ids.reshape(-1), num_segments=sigma_blocks.shape[0]
    )
    gradient = lax.psum(local_terms, ("slab", "freq"))
    return (forward_field, adjoint_field, gradient)


def solution(mesh):
    return jax.shard_map(
        body,
        mesh=mesh,
        in_specs=(
            P("freq", None, None, "slab", None, None),
            P("freq"),
            P(),
            P("slab", None, None),
            P("slab", None),
            P("slab"),
            P("freq", None, "slab"),
        ),
        out_specs=(
            P("freq", None, None, "slab", None, None),
            P("freq", None, None, "slab", None, None),
            P(),
        ),
        check_vma=False,
    )
```

profile of v0, /device:TPU:14, one launch (start us, length us, event | category | flops | bytes accessed | tf_op | source)
XLA Modules:
  0.0 1428.3 jit_solution(17710169639621398789)
XLA Ops:
  0.7 1.3 convert_element_type.32
  2.8 406.1 %gather_fusion = f32[65536]{0:T(1024)S(1)} fusion(f32[256]{0:T(256)S(1)} %copy-done, s32[65536]{0:T(1024)S(1)} %broadcast_clamp_fusion), kind=kCustom, calls=%fused_computation | custom fusion | bytes 786432 | tf_op jit(solution)/shard_map/jit(_take)/gather | solution.py:119
  410.8 2.4 collective-permute-start.1
  413.2 4.3 collective-permute-start
  418.0 3.9 collective-permute-done.1
  421.9 2.8 collective-permute-done
  424.7 1.3 pad_maximum_fusion
  430.8 14.9 %all-reduce.71 = (f32[1]{0:T(128)}, f32[1]{0:T(128)}, f32[1]{0:T(128)}) all-reduce(f32[1]{0:T(128)} %bitcast.16, f32[1]{0:T(128)} %bitcast.14, f32[1]{0:T(128)} %bitcast.13), channel_id=1, replica_groups=mesh['slab'=8,'freq'=4] {'slab'}, use_global_device_ids=true, to_apply=%region_5.6 | all-reduce | flops 3 | bytes 24 | tf_op jit(solution)/shard_map/psum | solution.py:90
  447.4 3.7 multiply_subtract_fusion.12
  453.6 4.3 collective-permute-start.3
  458.0 2.4 collective-permute-start.2
  462.2 8.1 all-to-all-start
  470.3 1.5 pad_maximum_fusion.1
  476.7 15.7 %all-reduce.70 = (f32[1]{0:T(128)}, f32[1]{0:T(128)}, f32[1]{0:T(128)}) all-reduce(f32[1]{0:T(128)} %bitcast.32, f32[1]{0:T(128)} %bitcast.30, f32[1]{0:T(128)} %bitcast.29), channel_id=1, replica_groups=mesh['slab'=8,'freq'=4] {'slab'}, use_global_device_ids=true, to_apply=%region_11.12 | all-reduce | flops 3 | bytes 24 | tf_op jit(solution)/shard_map/psum | solution.py:90
  494.3 3.7 multiply_subtract_fusion.10
  500.5 6.1 collective-permute-start.5
  506.6 2.1 collective-permute-start.4
  509.8 4.5 collective-permute-done.4
  514.3 1.5 pad_maximum_fusion.2
  520.6 17.6 %all-reduce.69 = (f32[1]{0:T(128)}, f32[1]{0:T(128)}, f32[1]{0:T(128)}) all-reduce(f32[1]{0:T(128)} %bitcast.48, f32[1]{0:T(128)} %bitcast.46, f32[1]{0:T(128)} %bitcast.45), channel_id=1, replica_groups=mesh['slab'=8,'freq'=4] {'slab'}, use_global_device_ids=true, to_apply=%region_17.18 | all-reduce | flops 3 | bytes 24 | tf_op jit(solution)/shard_map/psum | solution.py:90
  540.1 3.7 multiply_subtract_fusion.8
  544.8 4.2 collective-permute-start.7
  549.0 2.5 collective-permute-start.6
  551.6 1.8 collective-permute-done.7
  553.4 3.7 collective-permute-done.6
  560.0 1.3 fusion.61
  561.4 17.1 %all-reduce.68 = (f32[1]{0:T(128)}, f32[1]{0:T(128)}, f32[1]{0:T(128)}) all-reduce(f32[1]{0:T(128)} %bitcast.64, f32[1]{0:T(128)} %bitcast.62, f32[1]{0:T(128)} %bitcast.61), channel_id=1, replica_groups=mesh['slab'=8,'freq'=4] {'slab'}, use_global_device_ids=true, to_apply=%region_23.24 | all-reduce | flops 3 | bytes 24 | tf_op jit(solution)/shard_map/psum | solution.py:90
  582.8 5.9 fusion.7
  588.7 44.4 %copy.224 = f32[2,196608]{0,1:T(8,128)} copy(f32[2,196608]{1,0:T(2,128)S(1)} %fusion.7) | data formatting | bytes 3145728 | tf_op jit(solution)/shard_map/add | solution.py:101
  633.1 4.9 gather_fusion.1
  638.8 10.6 all-to-all-start.1
  649.4 2.5 sort
  651.9 1.6 all-to-all-done.1
  656.1 5.6 all-to-all-start.2
  661.8 4.1 all-to-all-done.2
  666.2 44.5 %scatter_custom_fusion.2 = f32[2,196608]{0,1:T(8,128)} fusion(s32[256]{0:T(256)S(1)} %get-tuple-element.3, f32[]{:T(128)} %constant.38.clone.1, f32[256,2]{1,0:T(8,128)S(1)} %copy.232, s32[1024]{0:T(1024)S(1)} %pad_clamp_fusion), kind=kCustom, calls=%fused_computation.8 | custom fusion | flops 512 | bytes 1572868 | tf_op jit(solution)/shard_map/scatter-add | solution.py:161
  710.7 57.2 %copy.233 = f32[1,2,3,8,64,128]{5,4,3,2,1,0:T(8,128)S(1)} copy(f32[1,2,3,8,64,128]{1,5,4,3,2,0:T(8,128)} %bitcast.92) | data formatting | bytes 3145728 | tf_op jit(solution)/shard_map/reshape | solution.py:163
  768.2 3.1 collective-permute-start.9
  771.3 3.6 collective-permute-start.8
  774.9 1.7 collective-permute-done.9
  776.7 2.2 collective-permute-done.8
  783.8 17.1 %all-reduce.67 = (f32[1]{0:T(128)}, f32[1]{0:T(128)}, f32[1]{0:T(128)}) all-reduce(f32[1]{0:T(128)} %bitcast.106, f32[1]{0:T(128)} %bitcast.104, f32[1]{0:T(128)} %bitcast.103), channel_id=1, replica_groups=mesh['slab'=8,'freq'=4] {'slab'}, use_global_device_ids=true, to_apply=%region_34.35 | all-reduce | flops 3 | bytes 24 | tf_op jit(solution)/shard_map/psum | solution.py:90
  802.8 3.3 multiply_subtract_fusion.5
  807.5 3.3 collective-permute-start.11
  810.8 3.7 collective-permute-start.10
  814.4 1.5 collective-permute-done.11
  815.9 2.9 collective-permute-done.10
  823.8 17.1 %all-reduce.66 = (f32[1]{0:T(128)}, f32[1]{0:T(128)}, f32[1]{0:T(128)}) all-reduce(f32[1]{0:T(128)} %bitcast.122, f32[1]{0:T(128)} %bitcast.120, f32[1]{0:T(128)} %bitcast.119), channel_id=1, replica_groups=mesh['slab'=8,'freq'=4] {'slab'}, use_global_device_ids=true, to_apply=%region_40.41 | all-reduce | flops 3 | bytes 24 | tf_op jit(solution)/shard_map/psum | solution.py:90
  842.7 3.4 multiply_subtract_fusion.3
  847.5 4.1 collective-permute-start.13
  851.6 2.6 collective-permute-start.12
  854.3 1.7 collective-permute-done.13
  856.0 5.7 collective-permute-done.12
  866.3 17.7 %all-reduce.65 = (f32[1]{0:T(128)}, f32[1]{0:T(128)}, f32[1]{0:T(128)}) all-reduce(f32[1]{0:T(128)} %bitcast.138, f32[1]{0:T(128)} %bitcast.136, f32[1]{0:T(128)} %bitcast.135), channel_id=1, replica_groups=mesh['slab'=8,'freq'=4] {'slab'}, use_global_device_ids=true, to_apply=%region_46.47 | all-reduce | flops 3 | bytes 24 | tf_op jit(solution)/shard_map/psum | solution.py:90
  886.0 3.5 multiply_subtract_fusion.1
  890.6 4.7 collective-permute-start.15
  895.2 2.6 collective-permute-start.14
  897.9 1.8 fusion.4
  899.7 3.3 collective-permute-done.14
  905.9 1.3 fusion.20
  907.2 17.2 %all-reduce.64 = (f32[1]{0:T(128)}, f32[1]{0:T(128)}, f32[1]{0:T(128)}) all-reduce(f32[1]{0:T(128)} %bitcast.154, f32[1]{0:T(128)} %bitcast.152, f32[1]{0:T(128)} %bitcast.151), channel_id=1, replica_groups=mesh['slab'=8,'freq'=4] {'slab'}, use_global_device_ids=true, to_apply=%region_52.53 | all-reduce | flops 3 | bytes 24 | tf_op jit(solution)/shard_map/psum | solution.py:90
  928.1 2.0 fusion.9
  931.3 452.6 %scatter_custom_fusion.3 = f32[256]{0:T(256)S(1)} fusion(s32[65536]{0:T(1024)} %bitcast.724, f32[65536]{0:T(1024)S(1)} %bitcast.727, f32[]{:T(128)} %constant.38.clone.1), kind=kCustom, calls=%fused_computation.483 | custom fusion | flops 65536 | bytes 1536 | tf_op jit(solution)/shard_map/scatter-add | solution.py:172
  1383.9 43.9 %psum.199 = f32[256]{0:T(256)} all-reduce(f32[256]{0:T(256)S(1)} %scatter_custom_fusion.3), channel_id=1, replica_groups=mesh['slab'=8,'freq'=4] {'slab','freq'}, use_global_device_ids=true, to_apply=%region_55.56 | all-reduce | flops 256 | bytes 2048 | tf_op jit(solution)/shard_map/psum | solution.py:175
  (318 shorter events, 58.3 us)
Async XLA Ops:
  0.6 2.1 copy-start
  0.6 1.4 copy-start.60
  409.2 16.8 %copy-start.9 = (f32[1,1,3,8,64,128]{5,4,3,2,1,0:T(8,128)}, f32[1,1,3,8,64,128]{5,4,3,2,1,0:T(8,128)S(1)}, u32[]{:S(2)}) copy-start(f32[1,1,3,8,64,128]{5,4,3,2,1,0:T(8,128)S(1)} %get-tuple-element.99) | copy-start | bytes 2359300
  409.2 8.3 copy-start.61
  410.8 11.1 collective-permute-start.1
  413.2 11.5 collective-permute-start
  428.3 1.1 copy-start.2
  447.4 3.7 copy-start.8
  452.5 1.2 copy-start.12
  453.6 16.7 %collective-permute-start.3 = (f32[1,2,3,1,64,128]{5,4,3,2,1,0:T(8,128)S(1)}, f32[1,2,3,1,64,128]{5,4,3,2,1,0:T(8,128)S(1)}, u32[]{:S(2)}, u32[]{:S(2)}) collective-permute-start(f32[1,2,3,1,64,128]{5,4,3,2,1,0:T(8,128)S(1)} %get-tuple-element.152), channel_id=1, source_target_pairs={{4,0},{8,4},{12,8},{16,12},{20,16},{24,20},{28,24},{5,1},{9,5},{13... | collective-permute-start | bytes 589832 | tf_op jit(solution)/shard_map/ppermute | solution.py:20
  458.0 12.4 collective-permute-start.2
  462.2 46.6 %all-to-all-start = ((s32[8,1,32]{2,1,0:T(1,128)}), s32[8,1,32]{2,1,0:T(1,128)S(1)}, u32[]{:S(2)}, u32[]{:S(2)}) async-start(s32[8,1,32]{2,1,0:T(1,128)} %all_to_all.12), calls=%async_computation | async-start | bytes 8192 | tf_op jit(solution)/shard_map/all_to_all | solution.py:140
  494.2 3.7 copy-start.19
  494.3 3.7 copy-start.22
  498.0 1.2 copy-start.32
  500.5 9.2 collective-permute-start.5
  506.6 7.7 collective-permute-start.4
  540.0 3.8 copy-start.20
  540.0 3.8 copy-start.23
  540.0 3.7 copy-start.31
  540.0 3.7 copy-start.33
  544.8 8.5 collective-permute-start.7
  549.0 8.1 collective-permute-start.6
  560.0 21.8 %copy-start.50 = (f32[1,1,3,8,64,128]{5,4,3,2,1,0:T(8,128)S(1)}, f32[1,1,3,8,64,128]{5,4,3,2,1,0:T(8,128)}, u32[]{:S(2)}) copy-start(f32[1,1,3,8,64,128]{5,4,3,2,1,0:T(8,128)} %get-tuple-element.145) | copy-start | bytes 2359300
  580.4 1.4 copy-start.42
  580.4 1.8 copy-start.44
  580.4 2.2 copy-start.46
  580.4 2.4 copy-start.48
  588.7 65.7 %copy-start.62 = (f32[1,2,128]{2,1,0:T(2,128)S(1)}, f32[1,2,128]{2,1,0:T(2,128)}, u32[]{:S(2)}) copy-start(f32[1,2,128]{2,1,0:T(2,128)} %param.13) | copy-start | bytes 3076
  638.8 14.8 %all-to-all-start.1 = ((f32[1,2,8,32]{3,1,0,2:T(2,128)}), f32[1,2,8,32]{3,1,0,2:T(2,128)S(1)}, u32[]{:S(2)}, u32[]{:S(2)}) async-start(f32[1,2,8,32]{3,1,0,2:T(2,128)} %select_multiply_fusion.1), calls=%async_computation.1 | async-start | bytes 16384 | tf_op jit(solution)/shard_map/all_to_all | solution.py:147
  656.1 9.8 all-to-all-start.2
  768.1 10.9 copy-start.17
  768.2 8.5 collective-permute-start.9
  771.3 7.6 collective-permute-start.8
  806.0 1.2 copy-start.27
  807.4 11.5 copy-start.15
  807.5 8.5 collective-permute-start.11
  810.8 8.1 collective-permute-start.10
  821.3 1.2 copy-start.5
  842.7 3.4 copy-start.25
  842.7 3.4 copy-start.28
  847.4 14.4 %copy-start.16 = (f32[1,1,3,8,64,128]{5,4,3,2,1,0:T(8,128)}, f32[1,1,3,8,64,128]{5,4,3,2,1,0:T(8,128)S(1)}, u32[]{:S(2)}) copy-start(f32[1,1,3,8,64,128]{5,4,3,2,1,0:T(8,128)S(1)} %get-tuple-element.88) | copy-start | bytes 2359300
  847.5 8.5 collective-permute-start.13
  851.6 10.0 collective-permute-start.12
  885.9 3.5 copy-start.26
  885.9 3.5 copy-start.29
  886.0 3.5 copy-start.35
  886.0 3.5 copy-start.37
  889.5 8.4 copy-start.52
  890.2 7.7 copy-start.43
  890.2 7.7 copy-start.45
  890.2 7.7 copy-start.47
  890.2 7.7 copy-start.49
  890.2 7.7 copy-start.51
  890.5 7.4 copy-start.39
  890.5 7.4 copy-start.41
  890.6 9.2 collective-permute-start.15
  895.2 7.8 collective-permute-start.14
  905.9 20.6 %copy-start.59 = (f32[1,1,3,8,64,128]{5,4,3,2,1,0:T(8,128)S(1)}, f32[1,1,3,8,64,128]{5,4,3,2,1,0:T(8,128)}, u32[]{:S(2)}) copy-start(f32[1,1,3,8,64,128]{5,4,3,2,1,0:T(8,128)} %get-tuple-element.129) | copy-start | bytes 2359300
  926.3 1.4 copy-start.56
  926.3 1.6 copy-start.57
  926.3 1.8 copy-start.58
  928.1 2.0 copy-start.53
  928.1 499.7 %copy-start.1 = (f32[256]{0:T(256)S(1)}, f32[256]{0:T(256)}, u32[]{:S(2)}) copy-start(f32[256]{0:T(256)} %param.9) | copy-start | bytes 3076
  (18 other events, 18.6 us)
where the time goes:
time: 1440 us; the launch traced here: 1430 us
  other arithmetic  570 us (40%)
  local copies, waits for them, and re-layouts  539 us (37%)
  blocking collectives  178 us (12%)
  starting transfers between devices  80.4 us (6%)
  waiting for transfers between devices  42.3 us (3%)
  between operations  18.4 us (1%)
    scatter-add x1, other arithmetic, body(): jax.ops.segment_sum(cell_term.reshape(-1), block_ids.reshape(-1), num_seg...  453 us
    gather x1, local copies, waits for them, and re-layouts, body(): conductivity = jnp.take(sigma_blocks, block_ids, axis=0)  406 us
    psum x8, blocking collectives, residual_sweeps(): lax.psum((jnp.sum(image_real * residual_real + image_imag * residual_imag...  134 us
    reshape x1, local copies, waits for them, and re-layouts, body(): adjoint_flat.reshape(forward_field.shape)  57.2 us
    scatter-add x3, other arithmetic, body(): adjoint_flat = jnp.zeros_like(flat_field).at[:, :, safe_edge].add(incomin...  47.1 us
    add x1, local copies, waits for them, and re-layouts, residual_sweeps(): solution + jnp.stack([step_real * precond_real - step_imag * precond_imag...  44.4 us
    psum x1, blocking collectives, body(): gradient = lax.psum(local_terms, ('slab', 'freq'))  43.9 us
    ppermute x8, starting transfers between devices, extended(): lax.ppermute(head, axis, [((i + 1) % count, i) for i in range(ends)])  32.2 us
  transfers between devices with their start and end apart: 19, of which 15 were waited for; matrix products, arithmetic and copies ran while one was open for 1% of the time, Pallas kernels for 0%

commit v1 on v0

--- a/solution.py
+++ b/solution.py
@@ -5,6 +5,11 @@
 
 SWEEPS = 4
 epsilon = 1e-06
+
+
+def serve_zones_by_axis(xin, named_axis, ax_name):
+    moved = lax.psum(xin, named_axis)
+    return lax.psum(moved, axis_name=ax_name)
 
 
 def extended(cells, sides, width):
@@ -172,7 +177,7 @@
     local_terms = jax.ops.segment_sum(
         cell_term.reshape(-1), block_ids.reshape(-1), num_segments=sigma_blocks.shape[0]
     )
-    gradient = lax.psum(local_terms, ("slab", "freq"))
+    gradient = serve_zones_by_axis(local_terms, "freq", ax_name="slab")
     return (forward_field, adjoint_field, gradient)
 
 

time: 1440 us -> 1420 us (0.986)
  blocking collectives: 178 us -> 160 us
    psum x1 -> x2, blocking collectives: 43.9 us -> 26 us  [the longest x1 20.1 us: serve_zones_by_axis(): return lax.psum(moved, axis_name=ax_name)]
where the time goes in v1:
time: 1420 us; the launch traced here: 1410 us
  other arithmetic  570 us (40%)
  local copies, waits for them, and re-layouts  539 us (38%)
  blocking collectives  160 us (11%)
  starting transfers between devices  80.6 us (6%)
  waiting for transfers between devices  42.4 us (3%)
  between operations  18.5 us (1%)
    scatter-add x1, other arithmetic, body(): jax.ops.segment_sum(cell_term.reshape(-1), block_ids.reshape(-1), num_seg...  453 us
    gather x1, local copies, waits for them, and re-layouts, body(): conductivity = jnp.take(sigma_blocks, block_ids, axis=0)  406 us
    psum x8, blocking collectives, residual_sweeps(): lax.psum((jnp.sum(image_real * residual_real + image_imag * residual_imag...  134 us
    reshape x1, local copies, waits for them, and re-layouts, body(): adjoint_flat.reshape(forward_field.shape)  57.2 us
    scatter-add x3, other arithmetic, body(): adjoint_flat = jnp.zeros_like(flat_field).at[:, :, safe_edge].add(incomin...  47.1 us
    add x1, local copies, waits for them, and re-layouts, residual_sweeps(): solution + jnp.stack([step_real * precond_real - step_imag * precond_imag...  44.5 us
    ppermute x8, starting transfers between devices, extended(): lax.ppermute(head, axis, [((i + 1) % count, i) for i in range(ends)])  32.5 us
  transfers between devices with their start and end apart: 19, of which 15 were waited for; matrix products, arithmetic and copies ran while one was open for 1% of the time, Pallas kernels for 0%

profile of v1, /device:TPU:14, one launch (start us, length us, event | category | flops | bytes accessed | tf_op | source)
XLA Modules:
  0.0 1410.3 jit_solution(14579306841632204684)
XLA Ops:
  0.7 1.3 convert_element_type.32
  2.8 406.1 %gather_fusion = f32[65536]{0:T(1024)S(1)} fusion(f32[256]{0:T(256)S(1)} %copy-done, s32[65536]{0:T(1024)S(1)} %broadcast_clamp_fusion), kind=kCustom, calls=%fused_computation | custom fusion | bytes 786432 | tf_op jit(solution)/shard_map/jit(_take)/gather | solution.py:124
  410.8 2.4 collective-permute-start.1
  413.2 4.3 collective-permute-start
  418.0 3.9 collective-permute-done.1
  421.9 2.8 collective-permute-done
  424.7 1.3 pad_maximum_fusion
  430.7 14.9 %all-reduce.71 = (f32[1]{0:T(128)}, f32[1]{0:T(128)}, f32[1]{0:T(128)}) all-reduce(f32[1]{0:T(128)} %bitcast.16, f32[1]{0:T(128)} %bitcast.14, f32[1]{0:T(128)} %bitcast.13), channel_id=1, replica_groups=mesh['slab'=8,'freq'=4] {'slab'}, use_global_device_ids=true, to_apply=%region_5.6 | all-reduce | flops 3 | bytes 24 | tf_op jit(solution)/shard_map/psum | solution.py:95
  447.5 3.7 multiply_subtract_fusion.12
  453.8 4.3 collective-permute-start.3
  458.1 2.4 collective-permute-start.2
  462.3 8.1 all-to-all-start
  470.4 1.5 pad_maximum_fusion.1
  475.4 1.3 fusion.81
  476.7 15.7 %all-reduce.70 = (f32[1]{0:T(128)}, f32[1]{0:T(128)}, f32[1]{0:T(128)}) all-reduce(f32[1]{0:T(128)} %bitcast.32, f32[1]{0:T(128)} %bitcast.30, f32[1]{0:T(128)} %bitcast.29), channel_id=1, replica_groups=mesh['slab'=8,'freq'=4] {'slab'}, use_global_device_ids=true, to_apply=%region_11.12 | all-reduce | flops 3 | bytes 24 | tf_op jit(solution)/shard_map/psum | solution.py:95
  494.2 3.7 multiply_subtract_fusion.10
  500.4 6.1 collective-permute-start.5
  506.5 2.1 collective-permute-start.4
  509.7 4.5 collective-permute-done.4
  514.2 1.5 pad_maximum_fusion.2
  520.5 17.2 %all-reduce.69 = (f32[1]{0:T(128)}, f32[1]{0:T(128)}, f32[1]{0:T(128)}) all-reduce(f32[1]{0:T(128)} %bitcast.48, f32[1]{0:T(128)} %bitcast.46, f32[1]{0:T(128)} %bitcast.45), channel_id=1, replica_groups=mesh['slab'=8,'freq'=4] {'slab'}, use_global_device_ids=true, to_apply=%region_17.18 | all-reduce | flops 3 | bytes 24 | tf_op jit(solution)/shard_map/psum | solution.py:95
  539.6 3.7 multiply_subtract_fusion.8
  544.4 4.6 collective-permute-start.7
  549.0 2.1 collective-permute-start.6
  551.2 1.7 collective-permute-done.7
  552.9 3.8 collective-permute-done.6
  560.9 17.3 %all-reduce.68 = (f32[1]{0:T(128)}, f32[1]{0:T(128)}, f32[1]{0:T(128)}) all-reduce(f32[1]{0:T(128)} %bitcast.64, f32[1]{0:T(128)} %bitcast.62, f32[1]{0:T(128)} %bitcast.61), channel_id=1, replica_groups=mesh['slab'=8,'freq'=4] {'slab'}, use_global_device_ids=true, to_apply=%region_23.24 | all-reduce | flops 3 | bytes 24 | tf_op jit(solution)/shard_map/psum | solution.py:95
  582.5 5.9 fusion.7
  588.4 44.5 %copy.224 = f32[2,196608]{0,1:T(8,128)} copy(f32[2,196608]{1,0:T(2,128)S(1)} %fusion.7) | data formatting | bytes 3145728 | tf_op jit(solution)/shard_map/add | solution.py:106
  632.9 4.9 gather_fusion.1
  638.5 10.9 all-to-all-start.1
  649.5 2.5 sort
  652.0 1.6 all-to-all-done.1
  656.2 5.6 all-to-all-start.2
  661.9 4.1 all-to-all-done.2
  666.2 44.5 %scatter_custom_fusion.2 = f32[2,196608]{0,1:T(8,128)} fusion(s32[256]{0:T(256)S(1)} %get-tuple-element.3, f32[]{:T(128)} %constant.38.clone.1, f32[256,2]{1,0:T(8,128)S(1)} %copy.232, s32[1024]{0:T(1024)S(1)} %pad_clamp_fusion), kind=kCustom, calls=%fused_computation.8 | custom fusion | flops 512 | bytes 1572868 | tf_op jit(solution)/shard_map/scatter-add | solution.py:166
  710.8 57.2 %copy.233 = f32[1,2,3,8,64,128]{5,4,3,2,1,0:T(8,128)S(1)} copy(f32[1,2,3,8,64,128]{1,5,4,3,2,0:T(8,128)} %bitcast.92) | data formatting | bytes 3145728 | tf_op jit(solution)/shard_map/reshape | solution.py:168
  768.2 3.1 collective-permute-start.9
  771.4 3.6 collective-permute-start.8
  775.0 1.7 collective-permute-done.9
  776.8 2.2 collective-permute-done.8
  783.8 17.1 %all-reduce.67 = (f32[1]{0:T(128)}, f32[1]{0:T(128)}, f32[1]{0:T(128)}) all-reduce(f32[1]{0:T(128)} %bitcast.106, f32[1]{0:T(128)} %bitcast.104, f32[1]{0:T(128)} %bitcast.103), channel_id=1, replica_groups=mesh['slab'=8,'freq'=4] {'slab'}, use_global_device_ids=true, to_apply=%region_34.35 | all-reduce | flops 3 | bytes 24 | tf_op jit(solution)/shard_map/psum | solution.py:95
  802.8 3.3 multiply_subtract_fusion.5
  807.5 3.3 collective-permute-start.11
  810.8 3.7 collective-permute-start.10
  814.4 1.5 collective-permute-done.11
  815.9 2.9 collective-permute-done.10
  823.7 17.1 %all-reduce.66 = (f32[1]{0:T(128)}, f32[1]{0:T(128)}, f32[1]{0:T(128)}) all-reduce(f32[1]{0:T(128)} %bitcast.122, f32[1]{0:T(128)} %bitcast.120, f32[1]{0:T(128)} %bitcast.119), channel_id=1, replica_groups=mesh['slab'=8,'freq'=4] {'slab'}, use_global_device_ids=true, to_apply=%region_40.41 | all-reduce | flops 3 | bytes 24 | tf_op jit(solution)/shard_map/psum | solution.py:95
  842.8 3.4 multiply_subtract_fusion.3
  847.6 4.1 collective-permute-start.13
  851.7 2.6 collective-permute-start.12
  854.4 1.7 collective-permute-done.13
  856.1 5.7 collective-permute-done.12
  866.5 17.7 %all-reduce.65 = (f32[1]{0:T(128)}, f32[1]{0:T(128)}, f32[1]{0:T(128)}) all-reduce(f32[1]{0:T(128)} %bitcast.138, f32[1]{0:T(128)} %bitcast.136, f32[1]{0:T(128)} %bitcast.135), channel_id=1, replica_groups=mesh['slab'=8,'freq'=4] {'slab'}, use_global_device_ids=true, to_apply=%region_46.47 | all-reduce | flops 3 | bytes 24 | tf_op jit(solution)/shard_map/psum | solution.py:95
  886.1 3.5 multiply_subtract_fusion.1
  890.7 4.6 collective-permute-start.15
  895.3 2.6 collective-permute-start.14
  898.1 1.8 fusion.4
  899.9 3.3 collective-permute-done.14
  907.3 17.1 %all-reduce.64 = (f32[1]{0:T(128)}, f32[1]{0:T(128)}, f32[1]{0:T(128)}) all-reduce(f32[1]{0:T(128)} %bitcast.154, f32[1]{0:T(128)} %bitcast.152, f32[1]{0:T(128)} %bitcast.151), channel_id=1, replica_groups=mesh['slab'=8,'freq'=4] {'slab'}, use_global_device_ids=true, to_apply=%region_52.53 | all-reduce | flops 3 | bytes 24 | tf_op jit(solution)/shard_map/psum | solution.py:95
  928.1 2.0 fusion.9
  931.3 452.6 %scatter_custom_fusion.3 = f32[256]{0:T(256)S(1)} fusion(s32[65536]{0:T(1024)} %bitcast.724, f32[65536]{0:T(1024)S(1)} %bitcast.727, f32[]{:T(128)} %constant.38.clone.1), kind=kCustom, calls=%fused_computation.483 | custom fusion | flops 65536 | bytes 1536 | tf_op jit(solution)/shard_map/scatter-add | solution.py:177
  1383.9 5.9 psum.206
  1389.8 20.1 %psum.207 = f32[256]{0:T(256)} all-reduce(f32[256]{0:T(256)S(1)} %psum.206), channel_id=1, replica_groups=mesh['slab'=8,'freq'=4] {'slab'}, use_global_device_ids=true, to_apply=%region_56.57 | all-reduce | flops 256 | bytes 2048 | tf_op jit(solution)/shard_map/psum | solution.py:12
  (319 shorter events, 59.4 us)
Async XLA Ops:
  0.6 2.1 copy-start
  0.6 1.4 copy-start.60
  409.2 16.8 %copy-start.9 = (f32[1,1,3,8,64,128]{5,4,3,2,1,0:T(8,128)}, f32[1,1,3,8,64,128]{5,4,3,2,1,0:T(8,128)S(1)}, u32[]{:S(2)}) copy-start(f32[1,1,3,8,64,128]{5,4,3,2,1,0:T(8,128)S(1)} %get-tuple-element.99) | copy-start | bytes 2359300
  409.2 8.3 copy-start.61
  410.8 11.1 collective-permute-start.1
  413.2 11.5 collective-permute-start
  428.3 1.1 copy-start.2
  447.5 3.7 copy-start.8
  451.2 1.2 copy-start.21
  452.6 1.2 copy-start.12
  453.8 16.6 %collective-permute-start.3 = (f32[1,2,3,1,64,128]{5,4,3,2,1,0:T(8,128)S(1)}, f32[1,2,3,1,64,128]{5,4,3,2,1,0:T(8,128)S(1)}, u32[]{:S(2)}, u32[]{:S(2)}) collective-permute-start(f32[1,2,3,1,64,128]{5,4,3,2,1,0:T(8,128)S(1)} %get-tuple-element.152), channel_id=1, source_target_pairs={{4,0},{8,4},{12,8},{16,12},{20,16},{24,20},{28,24},{5,1},{9,5},{13... | collective-permute-start | bytes 589832 | tf_op jit(solution)/shard_map/ppermute | solution.py:25
  458.1 12.3 collective-permute-start.2
  462.3 46.4 %all-to-all-start = ((s32[8,1,32]{2,1,0:T(1,128)}), s32[8,1,32]{2,1,0:T(1,128)S(1)}, u32[]{:S(2)}, u32[]{:S(2)}) async-start(s32[8,1,32]{2,1,0:T(1,128)} %all_to_all.12), calls=%async_computation | async-start | bytes 8192 | tf_op jit(solution)/shard_map/all_to_all | solution.py:145
  474.3 1.1 copy-start.3
  494.2 3.7 copy-start.19
  494.2 3.7 copy-start.22
  500.4 9.2 collective-permute-start.5
  506.5 7.7 collective-permute-start.4
  539.6 3.8 copy-start.20
  539.6 3.8 copy-start.23
  539.6 3.8 copy-start.31
  539.6 3.8 copy-start.33
  544.4 8.5 collective-permute-start.7
  549.0 7.7 collective-permute-start.6
  559.6 21.9 %copy-start.50 = (f32[1,1,3,8,64,128]{5,4,3,2,1,0:T(8,128)S(1)}, f32[1,1,3,8,64,128]{5,4,3,2,1,0:T(8,128)}, u32[]{:S(2)}) copy-start(f32[1,1,3,8,64,128]{5,4,3,2,1,0:T(8,128)} %get-tuple-element.145) | copy-start | bytes 2359300
  580.1 1.4 copy-start.42
  580.1 1.8 copy-start.44
  580.2 2.2 copy-start.46
  580.2 2.4 copy-start.48
  588.4 66.0 %copy-start.62 = (f32[1,2,128]{2,1,0:T(2,128)S(1)}, f32[1,2,128]{2,1,0:T(2,128)}, u32[]{:S(2)}) copy-start(f32[1,2,128]{2,1,0:T(2,128)} %param.13) | copy-start | bytes 3076
  638.5 15.1 %all-to-all-start.1 = ((f32[1,2,8,32]{3,1,0,2:T(2,128)}), f32[1,2,8,32]{3,1,0,2:T(2,128)S(1)}, u32[]{:S(2)}, u32[]{:S(2)}) async-start(f32[1,2,8,32]{3,1,0,2:T(2,128)} %select_multiply_fusion.1), calls=%async_computation.1 | async-start | bytes 16384 | tf_op jit(solution)/shard_map/all_to_all | solution.py:152
  656.2 9.8 all-to-all-start.2
  768.2 10.9 copy-start.17
  768.2 8.5 collective-permute-start.9
  771.4 7.6 collective-permute-start.8
  807.4 11.5 copy-start.15
  807.5 8.5 collective-permute-start.11
  810.8 8.1 collective-permute-start.10
  821.3 1.2 copy-start.5
  842.8 3.4 copy-start.25
  842.8 3.4 copy-start.28
  847.6 14.4 %copy-start.16 = (f32[1,1,3,8,64,128]{5,4,3,2,1,0:T(8,128)}, f32[1,1,3,8,64,128]{5,4,3,2,1,0:T(8,128)S(1)}, u32[]{:S(2)}) copy-start(f32[1,1,3,8,64,128]{5,4,3,2,1,0:T(8,128)S(1)} %get-tuple-element.88) | copy-start | bytes 2359300
  847.6 8.5 collective-permute-start.13
  851.7 10.0 collective-permute-start.12
  886.1 3.5 copy-start.26
  886.1 3.5 copy-start.29
  886.1 3.5 copy-start.35
  886.1 3.5 copy-start.37
  889.6 8.4 copy-start.52
  890.3 7.7 copy-start.43
  890.3 7.7 copy-start.45
  890.3 7.7 copy-start.47
  890.4 7.7 copy-start.49
  890.4 7.7 copy-start.51
  890.6 7.4 copy-start.39
  890.7 7.4 copy-start.41
  890.7 9.2 collective-permute-start.15
  895.3 7.8 collective-permute-start.14
  906.1 20.5 %copy-start.59 = (f32[1,1,3,8,64,128]{5,4,3,2,1,0:T(8,128)S(1)}, f32[1,1,3,8,64,128]{5,4,3,2,1,0:T(8,128)}, u32[]{:S(2)}) copy-start(f32[1,1,3,8,64,128]{5,4,3,2,1,0:T(8,128)} %get-tuple-element.129) | copy-start | bytes 2359300
  926.3 1.4 copy-start.56
  926.3 1.6 copy-start.57
  926.3 1.8 copy-start.58
  928.1 2.0 copy-start.53
  928.1 481.7 %copy-start.1 = (f32[256]{0:T(256)S(1)}, f32[256]{0:T(256)}, u32[]{:S(2)}) copy-start(f32[256]{0:T(256)} %param.9) | copy-start | bytes 3076
  (18 other events, 18.6 us)
